TPU v7x, 32 devices: a whole 2x2x4 slice. The times are simulated.
32 devices in a mesh: seq: 8 (over z, x), tensor: 4 (over y, core).
Axes of the slice: x: 2, y: 2, z: 4, core: 2. Of those that a mesh axis runs over, the one named last changes fastest.
Arguments:
- queries: bfloat16 [512, 2048], P('seq', 'tensor'), may hold values from -5 to 5
- draft_keys: bfloat16 [512, 2048], P('seq', 'tensor'), may hold values from -5 to 5
- draft_values: bfloat16 [512, 2048], P('seq', 'tensor'), may hold values from -6 to 6
- key_cache: bfloat16 [96, 128, 2048], P('seq', None, 'tensor'), may hold values from -6 to 6
- value_cache: bfloat16 [96, 128, 2048], P('seq', None, 'tensor'), may hold values from -6 to 6
- page_request: int32 [96], P('seq'), may hold values from 0 to 7, as said below
- page_slot: int32 [96], P('seq'), may hold values from 0 to 88, as said below
- cache_len: int32 [8], replicated, may hold values from 1 to 11384, as said below
- tree_mask: int32 [8, 64, 64], P('seq'), may hold values from 0 to 1, as said below
- accepted: int32 [8, 8], P('seq'), may hold values from 0 to 28, as said below
- hidden_in: bfloat16 [512, 2048], P('seq'), may hold values from -0.75 to 0.75
- out_proj: bfloat16 [2048, 2048], P('tensor'), may hold values from -0.125 to 0.125
- norm_gain: float32 [2048], replicated, may hold values from 0.5 to 1.5
- gate_proj: bfloat16 [64, 2048, 1024], P('seq', None, 'tensor'), may hold values from -0.125 to 0.125
- up_proj: bfloat16 [64, 2048, 1024], P('seq', None, 'tensor'), may hold values from -0.125 to 0.125
- down_proj: bfloat16 [64, 1024, 2048], P('seq', 'tensor'), may hold values from -0.1875 to 0.1875
- expert_ids: int32 [512, 8], P('seq'), may hold values from 0 to 63, all different within a row; in each aligned block of 64 rows (0 to 63, 64 to 127, ...) at most 16 rows name the same one
- route_weight: float32 [512, 8], P('seq'), may hold values from 0.02 to 0.5
Outputs:
- mixed_out: bfloat16 [512, 2048], P('seq', 'tensor')
- log_sum_exp: float32 [512, 16], P('seq', 'tensor')
- key_cache_out: bfloat16 [96, 128, 2048], P('seq', None, 'tensor')
- value_cache_out: bfloat16 [96, 128, 2048], P('seq', None, 'tensor')
Inputs may be any that keep to these rules, and one draw needn't show every extreme that they name: `page_request`: every request holds one or more pages and at most 128; together they hold all 96 pages, and one request holds min(128, 89). `page_slot`: the pages of one request carry the numbers 0, 1, 2 and so on, each once. A request's pages hold cache_len + 8 positions or more, and its last page holds at least one of its first cache_len positions. `tree_mask`: row i marks node i and its ancestors in a tree rooted at node 0; each node's parent stands one to four nodes before it. `accepted`: the 8 nodes nearest the root on a path from node 0, in order from the root. `expert_ids`: at most 16 of the 64 rows of one request name the same expert.
All inputs are finite; a program needn't handle non-finite values.
Results may differ from a plain program's by a relative error of at most 0.024.
Values may be sent and summed in bfloat16 or wider, within the bound.
No kernel may reach another device: no remote copies, remote signals or barrier semaphores. Data moves between devices by JAX's collectives and lax.ppermute only.
A program may use at most 128 MiB of HBM per device.

v0:
```python
import math
import jax
import jax.numpy as jnp
from jax import lax
from jax.sharding import PartitionSpec as P

HD = 128
EXPERTS = 64
CAP = 16
MASKED = -1e30
HIGHEST = lax.Precision.HIGHEST


def expert_block(slot_rows, gate_proj, up_proj, down_proj):
    gate_value = jnp.einsum(
        "gecd,edf->gecf", slot_rows, gate_proj, preferred_element_type=jnp.float32
    )
    up_value = jnp.einsum("gecd,edf->gecf", slot_rows, up_proj, preferred_element_type=jnp.float32)
    active = (jax.nn.silu(gate_value) * up_value).astype(jnp.bfloat16)
    return jnp.einsum(
        "gecf,efd->gecd", active, down_proj, preferred_element_type=jnp.float32
    ).astype(jnp.bfloat16)


def on_device(
    queries,
    draft_keys,
    draft_values,
    key_cache,
    value_cache,
    page_request,
    page_slot,
    cache_len,
    tree_mask,
    accepted,
    hidden_in,
    out_proj,
    norm_gain,
    gate_proj,
    up_proj,
    down_proj,
    expert_ids,
    route_weight,
):
    draft_len, head_width = queries.shape
    page_count, page_len, _ = key_cache.shape
    head_count = head_width // HD
    scaling = 1.0 / math.sqrt(HD)
    accept_rows = jnp.concatenate([draft_keys[accepted[0]], draft_values[accepted[0]]], axis=1)
    every_query, every_accept = (
        lax.all_gather(queries[None], "seq", axis=0, tiled=True),
        lax.all_gather(accept_rows[None], "seq", axis=0, tiled=True),
    )
    request_count = every_query.shape[0]
    request_ids = jnp.arange(request_count, dtype=jnp.int32)
    owner_mask = page_request[:, None] == request_ids[None, :]
    owner_weight = owner_mask.astype(jnp.bfloat16)
    page_queries = jnp.einsum(
        "pr,rqc->pqc", owner_weight, every_query, preferred_element_type=jnp.float32
    ).astype(jnp.bfloat16)
    page_length = jnp.sum(jnp.where(owner_mask, cache_len[None, :], 0), axis=1)
    position = page_slot[:, None] * page_len + jnp.arange(page_len, dtype=jnp.int32)[None, :]
    live_key = position < page_length[:, None]
    far_scores = (
        jnp.einsum(
            "pqhd,pkhd->phqk",
            page_queries.reshape(page_count, draft_len, head_count, HD),
            key_cache.reshape(page_count, page_len, head_count, HD),
            preferred_element_type=jnp.float32,
        )
        * scaling
    )
    far_scores = jnp.where(live_key[:, None, None, :], far_scores, MASKED)
    page_max = jnp.max(far_scores, axis=3)
    far_weights = jnp.exp(far_scores - page_max[:, :, :, None])
    page_sum = jnp.sum(far_weights, axis=3)
    page_out = jnp.einsum(
        "phqk,pkhd->phqd",
        far_weights.astype(jnp.bfloat16),
        value_cache.reshape(page_count, page_len, head_count, HD),
        preferred_element_type=jnp.float32,
    )
    member_mask = owner_mask.T[:, :, None, None]
    dest_max = jnp.max(jnp.where(member_mask, page_max[None], MASKED), axis=1)
    factor = jnp.where(
        member_mask, jnp.exp(jnp.minimum(page_max[None] - dest_max[:, None], 0.0)), 0.0
    )
    dest_sum = jnp.einsum("rphq,phq->rhq", factor, page_sum, precision=HIGHEST)
    dest_out = jnp.einsum("rphq,phqd->rhqd", factor, page_out, precision=HIGHEST)
    got_out, got_max, got_sum = (
        lax.all_to_all(
            dest_out.astype(jnp.bfloat16), "seq", split_axis=0, concat_axis=0, tiled=True
        ).astype(dest_out.dtype),
        lax.all_to_all(
            dest_max.astype(jnp.bfloat16), "seq", split_axis=0, concat_axis=0, tiled=True
        ).astype(dest_max.dtype),
        lax.all_to_all(
            dest_sum.astype(jnp.bfloat16), "seq", split_axis=0, concat_axis=0, tiled=True
        ).astype(dest_sum.dtype),
    )
    own_queries = queries.reshape(draft_len, head_count, HD)
    near_scores = (
        jnp.einsum(
            "qhd,khd->hqk",
            own_queries,
            draft_keys.reshape(draft_len, head_count, HD),
            preferred_element_type=jnp.float32,
        )
        * scaling
    )
    near_scores = jnp.where((tree_mask[0] > 0)[None], near_scores, MASKED)
    near_max = jnp.max(near_scores, axis=2)
    near_weights = jnp.exp(near_scores - near_max[:, :, None])
    near_sum = jnp.sum(near_weights, axis=2)
    near_out = jnp.einsum(
        "hqk,khd->hqd",
        near_weights.astype(jnp.bfloat16),
        draft_values.reshape(draft_len, head_count, HD),
        preferred_element_type=jnp.float32,
    )
    row_max = jnp.maximum(near_max, jnp.max(got_max, axis=0))
    near_scale = jnp.exp(near_max - row_max)
    far_scale = jnp.exp(got_max - row_max[None])
    total_sum = near_sum * near_scale + jnp.sum(got_sum * far_scale, axis=0)
    summed = near_out * near_scale[:, :, None] + jnp.sum(got_out * far_scale[:, :, :, None], axis=0)
    attended = (
        (summed / total_sum[:, :, None])
        .transpose(1, 0, 2)
        .reshape(draft_len, head_width)
        .astype(jnp.bfloat16)
    )
    log_sum_exp = (row_max + jnp.log(total_sum)).T
    partial_proj = jnp.dot(attended, out_proj, preferred_element_type=jnp.float32)
    projected = lax.psum(partial_proj.astype(jnp.bfloat16), "tensor").astype(jnp.float32)
    mixed = hidden_in.astype(jnp.float32) + projected
    normed = (
        mixed * lax.rsqrt(jnp.mean(mixed * mixed, axis=1, keepdims=True) + 1e-06) * norm_gain
    ).astype(jnp.bfloat16)
    pick_count = expert_ids.shape[1]
    local_experts = gate_proj.shape[0]
    group_count = EXPERTS // local_experts
    slots_total = EXPERTS * CAP
    flat_ids = expert_ids.reshape(-1)
    hits = (flat_ids[:, None] == jnp.arange(EXPERTS, dtype=jnp.int32)[None, :]).astype(jnp.int32)
    rank = jnp.sum((jnp.cumsum(hits, axis=0) - hits) * hits, axis=1)
    slot_of = (flat_ids * CAP + rank).reshape(draft_len, pick_count)
    slot_ids = jnp.arange(slots_total, dtype=jnp.int32)
    dispatch_map = jnp.any(slot_ids[:, None, None] == slot_of[None], axis=2).astype(jnp.bfloat16)
    send_rows = (
        jnp.dot(dispatch_map, normed, preferred_element_type=jnp.float32)
        .astype(jnp.bfloat16)
        .reshape(group_count, local_experts, CAP, normed.shape[1])
    )
    combine = jnp.sum(
        jnp.where(slot_of[:, :, None] == slot_ids[None, None, :], route_weight[:, :, None], 0.0),
        axis=1,
    )
    column_width = mixed.shape[1] // lax.axis_size("tensor")
    column_start = lax.axis_index("tensor") * column_width
    result = expert_block(
        lax.all_to_all(send_rows, "seq", split_axis=0, concat_axis=0, tiled=True),
        gate_proj,
        up_proj,
        down_proj,
    )
    back_rows = lax.all_to_all(result, "seq", split_axis=0, concat_axis=0, tiled=True)
    flat_rows = back_rows.reshape(slots_total, back_rows.shape[3])
    combine_high = combine.astype(jnp.bfloat16)
    combine_low = (combine - combine_high.astype(jnp.float32)).astype(jnp.bfloat16)
    weighted = jnp.dot(combine_high, flat_rows, preferred_element_type=jnp.float32) + jnp.dot(
        combine_low, flat_rows, preferred_element_type=jnp.float32
    )
    moe_part = lax.psum_scatter(
        weighted.astype(jnp.bfloat16), "tensor", scatter_dimension=1, tiled=True
    ).astype(jnp.float32)
    mixed_out = (lax.dynamic_slice_in_dim(mixed, column_start, column_width, 1) + moe_part).astype(
        jnp.bfloat16
    )
    accept_count = every_accept.shape[1]
    page_accept = jnp.einsum(
        "pr,rac->pac", owner_weight, every_accept, preferred_element_type=jnp.float32
    ).astype(jnp.bfloat16)
    offset = position - page_length[:, None]
    placement = offset[:, :, None] == jnp.arange(accept_count, dtype=jnp.int32)[None, None, :]
    written = jnp.einsum(
        "pia,pac->pic",
        placement.astype(jnp.bfloat16),
        page_accept,
        preferred_element_type=jnp.float32,
    ).astype(jnp.bfloat16)
    touched = jnp.any(placement, axis=2)[:, :, None]
    key_cache_out = jnp.where(touched, written[:, :, :head_width], key_cache)
    value_cache_out = jnp.where(touched, written[:, :, head_width:], value_cache)
    return (mixed_out, log_sum_exp, key_cache_out, value_cache_out)


def solution(mesh):
    return jax.shard_map(
        on_device,
        mesh=mesh,
        in_specs=(
            P("seq", "tensor"),
            P("seq", "tensor"),
            P("seq", "tensor"),
            P("seq", None, "tensor"),
            P("seq", None, "tensor"),
            P("seq"),
            P("seq"),
            P(),
            P("seq", None, None),
            P("seq", None),
            P("seq", None),
            P("tensor", None),
            P(),
            P("seq", None, "tensor"),
            P("seq", None, "tensor"),
            P("seq", "tensor", None),
            P("seq", None),
            P("seq", None),
        ),
        out_specs=(
            P("seq", "tensor"),
            P("seq", "tensor"),
            P("seq", None, "tensor"),
            P("seq", None, "tensor"),
        ),
        check_vma=False,
    )
```

profile of v0, /device:TPU:0, one launch (start us, length us, event | category | flops | bytes accessed | tf_op | source)
XLA Modules:
  0.0 393.0 jit_solution(8291172530403849364)
XLA Ops:
  7.2 0.8 broadcast_multiply_fusion
  8.0 0.7 iota_compare_fusion.7
  8.6 0.8 select_reduce_fusion.2
  9.4 33.2 %all-gather = bf16[512,512]{1,0:T(8,128)(2,1)S(1)} all-gather(bf16[64,512]{1,0:T(8,128)(2,1)} %param.18), channel_id=2, replica_groups=mesh['seq'=8,'tensor'=4] {'seq'}, dimensions={0}, use_global_device_ids=true | all-gather | bytes 589824 | tf_op jit(solution)/shard_map/all_gather | solution.py:51
  42.6 1.2 convolution_convert_fusion.3
  43.8 1.3 reshape.247
  45.1 0.1 fusion.90
  45.1 4.0 %fusion.103 = (f32[12,4,64]{2,1,0:T(4,128)S(1)}, f32[12,4,64,128]{3,2,1,0:T(8,128)}) fusion(bf16[12,64,4,128]{3,2,0,1:T(4,128)(2,1)} %reshape.247, pred[12,128]{1,0:T(8,128)(4,1)S(1)} %fusion.90, bf16[12,128,512]{2,1,0:T(8,128)(2,1)} %param.21), kind=kOutput, calls=%fused_computation.125 | convolution fusion | flops 101839872 | bytes 3945984 | tf_op jit(solution)/shard_map/pqhd,pkhd->phqk/dot_general | solution.py:65
  49.1 0.1 copy.165
  49.2 2.3 fusion.22
  51.6 0.1 copy.197
  51.7 0.3 select_reduce_fusion.1
  52.0 0.7 multiply_reduce_fusion
  52.7 0.1 copy.206
  52.8 0.7 reshape.251
  53.5 5.7 %all-to-all-start.2 = ((bf16[8,2,128]{2,1,0:T(2,128)(2,1)}), bf16[8,2,128]{2,1,0:T(2,128)(2,1)S(1)}, u32[]{:S(2)}, u32[]{:S(2)}) async-start(bf16[8,2,128]{2,1,0:T(2,128)(2,1)} %reshape.251), calls=%async_computation.2 | async-start | bytes 8192 | tf_op jit(solution)/shard_map/all_to_all | solution.py:97
  59.2 0.1 copy.172
  59.3 0.1 eq.98
  59.3 0.1 eq.94
  59.5 2.5 fusion.14
  62.0 3.2 fusion.47
  65.2 1.2 reduce-window.6
  66.4 0.2 slice_reduce_fusion
  66.7 0.1 fusion.69
  66.8 0.1 copy.166
  66.9 0.7 reshape.249
  67.6 0.1 reduce_sum.89
  67.8 6.0 %all-to-all-start = ((bf16[8,2,128]{2,1,0:T(2,128)(2,1)}), bf16[8,2,128]{2,1,0:T(2,128)(2,1)S(1)}, u32[]{:S(2)}, u32[]{:S(2)}) async-start(bf16[8,2,128]{2,1,0:T(2,128)(2,1)} %reshape.249), calls=%async_computation | async-start | bytes 8192 | tf_op jit(solution)/shard_map/all_to_all | solution.py:94
  73.8 0.1 copy.156
  73.9 0.9 copy.170
  74.8 0.1 copy.176
  74.9 5.4 %all-to-all-done = bf16[8,2,128]{2,1,0:T(2,128)(2,1)S(1)} async-done(((bf16[8,2,128]{2,1,0:T(2,128)(2,1)}), bf16[8,2,128]{2,1,0:T(2,128)(2,1)S(1)}, u32[]{:S(2)}, u32[]{:S(2)}) %all-to-all-start) | async-done | bytes 4128 | tf_op jit(solution)/shard_map/all_to_all | solution.py:94
  80.3 3.5 all-to-all-start.1
  83.8 0.2 fusion.104
  84.1 0.1 reshape.250
  84.2 0.1 reshape.252
  84.3 0.6 fusion.95
  84.9 9.1 %all-to-all-done.1 = bf16[8,4,64,128]{3,2,1,0:T(8,128)(2,1)S(1)} async-done(((bf16[8,4,64,128]{3,2,1,0:T(8,128)(2,1)}), bf16[8,4,64,128]{3,2,1,0:T(8,128)(2,1)S(1)}, u32[]{:S(2)}, u32[]{:S(2)}) %all-to-all-start.1) | async-done | bytes 524320 | tf_op jit(solution)/shard_map/all_to_all | solution.py:91
  94.0 0.3 multiply_reduce_fusion.1
  94.3 0.2 fusion.55
  94.6 1.2 convolution_convert_fusion.1
  95.8 0.7 fusion.13
  96.5 30.5 %all-reduce.2.cloned.1.call-done = bf16[64,2048]{1,0:T(8,128)(2,1)} async-done(((bf16[64,2048]{1,0:T(8,128)(2,1)}), bf16[64,2048]{1,0:T(8,128)(2,1)}) %all-reduce.2.cloned.1.call-update) | async-done | bytes 262160 | tf_op jit(solution)/shard_map/psum | solution.py:134
  127.0 1.1 convert_add_fusion
  128.2 2.4 convolution_convert_fusion
  130.6 97.6 %all_to_all.25 = bf16[8,8,16,2048]{3,2,1,0:T(8,128)(2,1)S(1)} all-to-all(bf16[8,8,16,2048]{3,2,1,0:T(8,128)(2,1)S(1)} %bitcast.166), channel_id=1, replica_groups=mesh['seq'=8,'tensor'=4] {'seq'}, dimensions={0} | all-to-all | bytes 8388608 | tf_op jit(solution)/shard_map/all_to_all | solution.py:161
  228.3 1.3 fusion.24
  229.5 5.0 %fusion.39 = bf16[8,8,16,256]{3,2,0,1:T(8,128)(2,1)S(1)} fusion(bf16[8,2048,256]{2,1,0:T(8,128)(2,1)} %param.32, bf16[8,8,16,2048]{3,2,1,0:T(8,128)(2,1)S(1)} %all_to_all.25, f32[8,8,16,256]{3,2,0,1:T(8,128)S(1)} %fusion.24), kind=kOutput, calls=%fused_computation.38 | convolution fusion | flops 1075314688 | bytes 14155776 | tf_op jit(solution)/shard_map/gecd,edf->gecf/dot_general | solution.py:18
  234.6 1.3 convert_bitcast_fusion
  235.8 2.5 copy.181
  238.3 4.7 %all-to-all-start.4 = ((bf16[8,8,16,2048]{3,2,1,0:T(8,128)(2,1)}), bf16[8,8,16,2048]{3,2,1,0:T(8,128)(2,1)}, u32[]{:S(2)}, u32[]{:S(2)}) async-start(bf16[8,8,16,2048]{3,2,1,0:T(8,128)(2,1)} %copy.181), calls=%async_computation.4 | async-start | bytes 8388608 | tf_op jit(solution)/shard_map/all_to_all | solution.py:166
  243.1 0.6 gather_fusion
  243.7 0.6 gather_fusion.1
  244.3 0.1 copy.177
  244.3 110.9 %all-gather.1 = bf16[64,1024]{1,0:T(8,128)(2,1)S(1)} all-gather(bf16[8,1024]{1,0:T(8,128)(2,1)S(1)} %pad_maximum_fusion), channel_id=3, replica_groups=mesh['seq'=8,'tensor'=4] {'seq'}, dimensions={0}, use_global_device_ids=true | all-gather | bytes 147456 | tf_op jit(solution)/shard_map/all_gather | solution.py:52
  355.2 0.7 select_reduce_fusion
  355.9 0.1 fusion.89
  356.0 0.3 convolution_convert_fusion.4
  356.3 2.8 convolution_convert_fusion.2
  359.1 3.0 fusion.84
  362.1 3.7 fusion.10
  365.9 4.3 %slice_select_fusion = (bf16[12,128,512]{2,1,0:T(8,128)(2,1)}, bf16[12,128,512]{2,1,0:T(8,128)(2,1)}) fusion(bf16[12,128,512]{2,1,0:T(8,128)(2,1)} %param.22, bf16[12,128,1024]{2,1,0:T(8,128)(2,1)} %convolution_convert_fusion.2, pred[12,128]{1,0:T(8,128)(4,1)S(1)} %fusion.87, bf16[12,128,512]{2,1,0:T(8,128)(2,1)} %param.21), kind=kLoop, calls=%fused_computation.28 | loop fusion | flops 1572864 | bytes 9438720 | tf_op jit(solution)/shard_map/jit(_where)/select_n | solution.py:193
  370.2 14.5 %reduce-scatter.2.cloned.1.call-done = bf16[64,512]{1,0:T(8,128)(2,1)} async-done(((bf16[64,2048]{1,0:T(8,128)(2,1)}), bf16[64,512]{1,0:T(8,128)(2,1)}) %reduce-scatter.2.cloned.1.call-update) | async-done | bytes 65552 | tf_op jit(solution)/shard_map/reduce_scatter | solution.py:173
  384.7 1.5 add_convert_fusion
  (56 shorter events, 0.5 us)
Async XLA Ops:
  7.2 87.4 %copy-start = (bf16[512,2048]{1,0:T(8,128)(2,1)S(1)}, bf16[512,2048]{1,0:T(8,128)(2,1)}, u32[]{:S(2)}) copy-start(bf16[512,2048]{1,0:T(8,128)(2,1)} %param.29) | copy-start | bytes 6291460
  49.1 10.0 %copy-start.7 = (s32[64,8]{0,1:T(8,128)S(1)}, s32[64,8]{0,1:T(8,128)}, u32[]{:S(2)}) copy-start(s32[64,8]{0,1:T(8,128)} %param.34) | copy-start | bytes 6148
  49.1 10.3 %copy-start.6 = (s32[1,64,64]{2,1,0:T(8,128)S(1)}, s32[1,64,64]{2,1,0:T(8,128)}, u32[]{:S(2)}) copy-start(s32[1,64,64]{2,1,0:T(8,128)} %param.26) | copy-start | bytes 49156
  53.5 14.3 %all-to-all-start.2 = ((bf16[8,2,128]{2,1,0:T(2,128)(2,1)}), bf16[8,2,128]{2,1,0:T(2,128)(2,1)S(1)}, u32[]{:S(2)}, u32[]{:S(2)}) async-start(bf16[8,2,128]{2,1,0:T(2,128)(2,1)} %reshape.251), calls=%async_computation.2 | async-start | bytes 8192 | tf_op jit(solution)/shard_map/all_to_all | solution.py:97
  65.2 18.6 %copy-start.3 = (bf16[64,512]{1,0:T(8,128)(2,1)S(1)}, bf16[64,512]{1,0:T(8,128)(2,1)}, u32[]{:S(2)}) copy-start(bf16[64,512]{1,0:T(8,128)(2,1)} %param.18) | copy-start | bytes 196612
  65.2 18.6 %copy-start.4 = (bf16[64,512]{1,0:T(8,128)(2,1)S(1)}, bf16[64,512]{1,0:T(8,128)(2,1)}, u32[]{:S(2)}) copy-start(bf16[64,512]{1,0:T(8,128)(2,1)} %param.19) | copy-start | bytes 196612
  65.2 29.1 %copy-start.5 = (bf16[64,512]{1,0:T(8,128)(2,1)S(1)}, bf16[64,512]{1,0:T(8,128)(2,1)}, u32[]{:S(2)}) copy-start(bf16[64,512]{1,0:T(8,128)(2,1)} %param.20) | copy-start | bytes 196612
  67.8 12.5 %all-to-all-start = ((bf16[8,2,128]{2,1,0:T(2,128)(2,1)}), bf16[8,2,128]{2,1,0:T(2,128)(2,1)S(1)}, u32[]{:S(2)}, u32[]{:S(2)}) async-start(bf16[8,2,128]{2,1,0:T(2,128)(2,1)} %reshape.249), calls=%async_computation | async-start | bytes 8192 | tf_op jit(solution)/shard_map/all_to_all | solution.py:94
  80.3 13.7 %all-to-all-start.1 = ((bf16[8,4,64,128]{3,2,1,0:T(8,128)(2,1)}), bf16[8,4,64,128]{3,2,1,0:T(8,128)(2,1)S(1)}, u32[]{:S(2)}, u32[]{:S(2)}) async-start(bf16[8,4,64,128]{3,2,1,0:T(8,128)(2,1)} %copy.170), calls=%async_computation.1 | async-start | bytes 1048576 | tf_op jit(solution)/shard_map/all_to_all | solution.py:91
  83.8 43.3 %all-reduce.2.cloned.1.call-start = ((), (), s32[]{:S(2)}) async-start(), calls=%async_computation.6 | async-start | bytes 524288 | tf_op jit(solution)/shard_map/psum | solution.py:134
  84.3 42.8 %copy-start.2 = (bf16[64,2048]{1,0:T(8,128)(2,1)S(1)}, bf16[64,2048]{1,0:T(8,128)(2,1)}, u32[]{:S(2)}) copy-start(bf16[64,2048]{1,0:T(8,128)(2,1)} %param.28) | copy-start | bytes 786436
  94.3 33.9 %copy-start.8 = (f32[2048]{0:T(1024)S(1)}, f32[2048]{0:T(1024)}, u32[]{:S(2)}) copy-start(f32[2048]{0:T(1024)} %param.30) | copy-start | bytes 24580
  128.2 100.1 %slice-start.2 = ((s8[8388608]{0:T(1024)(128)(4,1)}), s8[4194304]{0:T(1024)(128)(4,1)S(1)}, s32[]{:S(2)}) async-start(s8[8388608]{0:T(1024)(128)(4,1)} %bitcast.173), calls=%async_computation.10 | async-start | bytes 8388608
  130.6 97.6 %slice-start.3 = ((s8[8388608]{0:T(1024)(128)(4,1)}), s8[4194304]{0:T(1024)(128)(4,1)S(1)}, s32[]{:S(2)}) async-start(s8[8388608]{0:T(1024)(128)(4,1)} %bitcast.173), calls=%async_computation.11 | async-start | bytes 8388608
  228.3 6.3 %slice-start = ((s8[8388608]{0:T(1024)(128)(4,1)}), s8[4194304]{0:T(1024)(128)(4,1)S(1)}, s32[]{:S(2)}) async-start(s8[8388608]{0:T(1024)(128)(4,1)} %bitcast.167), calls=%async_computation.8 | async-start | bytes 8388608
  229.5 5.0 %slice-start.1 = ((s8[8388608]{0:T(1024)(128)(4,1)}), s8[4194304]{0:T(1024)(128)(4,1)S(1)}, s32[]{:S(2)}) async-start(s8[8388608]{0:T(1024)(128)(4,1)} %bitcast.167), calls=%async_computation.9 | async-start | bytes 8388608
  238.3 4.7 %copy-start.11 = (s32[1,8]{1,0:T(1,128)S(1)}, s32[1,8]{1,0:T(1,128)}, u32[]{:S(2)}) copy-start(s32[1,8]{1,0:T(1,128)} %param.27) | copy-start | bytes 100
  238.3 5.9 %copy-start.9 = (f32[64,8]{0,1:T(8,128)S(1)}, f32[64,8]{0,1:T(8,128)}, u32[]{:S(2)}) copy-start(f32[64,8]{0,1:T(8,128)} %param.35) | copy-start | bytes 6148
  238.3 117.7 %copy-start.10 = (s32[12]{0:T(128)S(1)}, s32[12]{0:T(128)}, u32[]{:S(2)}) copy-start(s32[12]{0:T(128)} %param.23) | copy-start | bytes 148
  238.3 120.8 %all-to-all-start.4 = ((bf16[8,8,16,2048]{3,2,1,0:T(8,128)(2,1)}), bf16[8,8,16,2048]{3,2,1,0:T(8,128)(2,1)}, u32[]{:S(2)}, u32[]{:S(2)}) async-start(bf16[8,8,16,2048]{3,2,1,0:T(8,128)(2,1)} %copy.181), calls=%async_computation.4 | async-start | bytes 8388608 | tf_op jit(solution)/shard_map/all_to_all | solution.py:166
  243.0 141.7 %reduce-scatter.2.cloned.1.call-start = ((), (), s32[]{:S(2)}) async-start(), calls=%async_computation.7 | async-start | bytes 327680 | tf_op jit(solution)/shard_map/reduce_scatter | solution.py:173
  365.9 20.3 %copy-start.1 = (bf16[512,2048]{1,0:T(8,128)(2,1)S(1)}, bf16[512,2048]{1,0:T(8,128)(2,1)}, u32[]{:S(2)}) copy-start(bf16[512,2048]{1,0:T(8,128)(2,1)} %param.29) | copy-start | bytes 6291460
Sparse Core Ops, SparseCore 0:
  95.9 31.0 all-reduce.1
  366.0 18.6 reduce-scatter.1
where the time goes:
time: 394 us; the launch traced here: 393 us
  blocking collectives  242 us (61%)
  waiting for transfers between devices  59.5 us (15%)
  matrix products  32.2 us (8%)
  starting transfers between devices  19.9 us (5%)
  other arithmetic  16.5 us (4%)
  between operations  14.4 us (4%)
  local copies, waits for them, and re-layouts  8.74 us (2%)
    all_gather x1, blocking collectives, on_device(): lax.all_gather(accept_rows[None], 'seq', axis=0, tiled=True)  111 us
    all_to_all x1, blocking collectives, on_device(): lax.all_to_all(send_rows, 'seq', split_axis=0, concat_axis=0, tiled=True)  97.6 us
    all_gather x1, blocking collectives, on_device(): lax.all_gather(queries[None], 'seq', axis=0, tiled=True)  33.2 us
    psum x1, waiting for transfers between devices, on_device(): lax.psum(partial_proj.astype(jnp.bfloat16), 'tensor').astype(jnp.float32)  30.5 us
    reduce_scatter x1, waiting for transfers between devices, on_device(): lax.psum_scatter(weighted.astype(jnp.bfloat16), 'tensor', scatter_dimensi...  14.5 us
    all_to_all x1, waiting for transfers between devices, on_device(): lax.all_to_all(dest_out.astype(jnp.bfloat16), 'seq', split_axis=0, concat...  9.08 us
  transfers between devices with their start and end apart: 6, of which 4 were waited for; matrix products, arithmetic and copies ran while one was open for 5% of the time, Pallas kernels for 0%

commit v1 on v0

--- a/solution.py
+++ b/solution.py
@@ -131,7 +131,9 @@
     )
     log_sum_exp = (row_max + jnp.log(total_sum)).T
     partial_proj = jnp.dot(attended, out_proj, preferred_element_type=jnp.float32)
-    projected = lax.psum(partial_proj.astype(jnp.bfloat16), "tensor").astype(jnp.float32)
+    projected = jnp.sum(
+        jax.lax.all_gather(partial_proj.astype(jnp.bfloat16), axis_name="tensor"), axis=0
+    ).astype(jnp.float32)
     mixed = hidden_in.astype(jnp.float32) + projected
     normed = (
         mixed * lax.rsqrt(jnp.mean(mixed * mixed, axis=1, keepdims=True) + 1e-06) * norm_gain

time: 394 us -> 377 us (0.957)
  waiting for transfers between devices: 59.5 us -> 41.6 us
    psum x1 -> x0, waiting for transfers between devices: 30.5 us -> none  [on_device(): lax.psum(partial_proj.astype(jnp.bfloat16), 'tensor').astype(jnp.float32)]
    all_gather x0 -> x1, waiting for transfers between devices: none -> 13.1 us  [on_device(): jax.lax.all_gather(partial_proj.astype(jnp.bfloat16), axis_name='tensor')]
  transfers between devices with their start and end apart: 6 -> 6, of which waited for: 4 -> 4; matrix products, arithmetic and copies ran while one was open for 5% -> 6% of each run, Pallas kernels for 0% -> 0%
where the time goes in v1:
time: 377 us; the launch traced here: 376 us
  blocking collectives  244 us (65%)
  waiting for transfers between devices  41.6 us (11%)
  matrix products  31.1 us (8%)
  starting transfers between devices  19.9 us (5%)
  other arithmetic  17 us (5%)
  between operations  14.4 us (4%)
  local copies, waits for them, and re-layouts  8.76 us (2%)
    all_gather x1, blocking collectives, on_device(): lax.all_gather(accept_rows[None], 'seq', axis=0, tiled=True)  111 us
    all_to_all x1, blocking collectives, on_device(): lax.all_to_all(send_rows, 'seq', split_axis=0, concat_axis=0, tiled=True)  99.1 us
    all_gather x1, blocking collectives, on_device(): lax.all_gather(queries[None], 'seq', axis=0, tiled=True)  33.2 us
    reduce_scatter x1, waiting for transfers between devices, on_device(): lax.psum_scatter(weighted.astype(jnp.bfloat16), 'tensor', scatter_dimensi...  13.9 us
    all_gather x1, waiting for transfers between devices, on_device(): jax.lax.all_gather(partial_proj.astype(jnp.bfloat16), axis_name='tensor')  13.1 us
    all_to_all x1, waiting for transfers between devices, on_device(): lax.all_to_all(dest_out.astype(jnp.bfloat16), 'seq', split_axis=0, concat...  9.07 us
  transfers between devices with their start and end apart: 6, of which 4 were waited for; matrix products, arithmetic and copies ran while one was open for 6% of the time, Pallas kernels for 0%

profile of v1, /device:TPU:0, one launch (start us, length us, event | category | flops | bytes accessed | tf_op | source)
XLA Modules:
  0.0 376.3 jit_solution(9274206276186860830)
XLA Ops:
  7.2 0.8 broadcast_multiply_fusion
  8.0 0.7 iota_compare_fusion.7
  8.6 0.8 select_reduce_fusion.2
  9.4 33.2 %all-gather = bf16[512,512]{1,0:T(8,128)(2,1)S(1)} all-gather(bf16[64,512]{1,0:T(8,128)(2,1)} %param.18), channel_id=2, replica_groups=mesh['seq'=8,'tensor'=4] {'seq'}, dimensions={0}, use_global_device_ids=true | all-gather | bytes 589824 | tf_op jit(solution)/shard_map/all_gather | solution.py:51
  42.6 1.2 convolution_convert_fusion.3
  43.8 1.3 reshape.248
  45.1 0.1 fusion.90
  45.1 4.0 %fusion.103 = (f32[12,4,64]{2,1,0:T(4,128)S(1)}, f32[12,4,64,128]{3,2,1,0:T(8,128)}) fusion(bf16[12,64,4,128]{3,2,0,1:T(4,128)(2,1)} %reshape.248, pred[12,128]{1,0:T(8,128)(4,1)S(1)} %fusion.90, bf16[12,128,512]{2,1,0:T(8,128)(2,1)} %param.21), kind=kOutput, calls=%fused_computation.125 | convolution fusion | flops 101839872 | bytes 3945984 | tf_op jit(solution)/shard_map/pqhd,pkhd->phqk/dot_general | solution.py:65
  49.1 0.1 copy.165
  49.2 2.3 fusion.22
  51.6 0.1 copy.197
  51.7 0.3 select_reduce_fusion.1
  52.0 0.7 multiply_reduce_fusion
  52.7 0.1 copy.206
  52.8 0.7 reshape.252
  53.5 5.7 %all-to-all-start.2 = ((bf16[8,2,128]{2,1,0:T(2,128)(2,1)}), bf16[8,2,128]{2,1,0:T(2,128)(2,1)S(1)}, u32[]{:S(2)}, u32[]{:S(2)}) async-start(bf16[8,2,128]{2,1,0:T(2,128)(2,1)} %reshape.252), calls=%async_computation.2 | async-start | bytes 8192 | tf_op jit(solution)/shard_map/all_to_all | solution.py:97
  59.2 2.5 fusion.14
  61.7 3.2 fusion.47
  64.9 0.1 copy.166
  65.0 0.7 reshape.250
  65.7 6.0 %all-to-all-start = ((bf16[8,2,128]{2,1,0:T(2,128)(2,1)}), bf16[8,2,128]{2,1,0:T(2,128)(2,1)S(1)}, u32[]{:S(2)}, u32[]{:S(2)}) async-start(bf16[8,2,128]{2,1,0:T(2,128)(2,1)} %reshape.250), calls=%async_computation | async-start | bytes 8192 | tf_op jit(solution)/shard_map/all_to_all | solution.py:94
  71.7 0.1 copy.156
  71.8 0.9 copy.170
  72.7 5.4 %all-to-all-done = bf16[8,2,128]{2,1,0:T(2,128)(2,1)S(1)} async-done(((bf16[8,2,128]{2,1,0:T(2,128)(2,1)}), bf16[8,2,128]{2,1,0:T(2,128)(2,1)S(1)}, u32[]{:S(2)}, u32[]{:S(2)}) %all-to-all-start) | async-done | bytes 4128 | tf_op jit(solution)/shard_map/all_to_all | solution.py:94
  78.2 3.5 all-to-all-start.1
  81.7 0.2 fusion.104
  82.0 0.1 reshape.251
  82.1 0.1 reshape.253
  82.2 0.6 fusion.95
  82.8 9.1 %all-to-all-done.1 = bf16[8,4,64,128]{3,2,1,0:T(8,128)(2,1)S(1)} async-done(((bf16[8,4,64,128]{3,2,1,0:T(8,128)(2,1)}), bf16[8,4,64,128]{3,2,1,0:T(8,128)(2,1)S(1)}, u32[]{:S(2)}, u32[]{:S(2)}) %all-to-all-start.1) | async-done | bytes 524320 | tf_op jit(solution)/shard_map/all_to_all | solution.py:91
  91.9 0.3 multiply_reduce_fusion.1
  92.2 0.2 fusion.55
  92.5 1.2 convolution_convert_fusion.1
  93.7 0.1 copy.172
  93.8 0.1 eq.98
  93.9 0.1 eq.94
  94.0 1.2 reduce-window.6
  95.2 0.2 slice_reduce_fusion
  95.5 0.1 fusion.69
  95.6 0.1 reduce_sum.102
  95.8 0.1 copy.176
  95.9 0.7 fusion.13
  96.6 13.1 %all-gather.5.cloned.1.call-done = bf16[256,2048]{1,0:T(8,128)(2,1)} async-done(((bf16[64,2048]{1,0:T(8,128)(2,1)}), bf16[256,2048]{1,0:T(8,128)(2,1)}) %all-gather.5.cloned.1.call-update) | async-done | bytes 1048592 | tf_op jit(solution)/shard_map/all_gather | solution.py:135
  109.7 1.4 reduce_sum.100
  111.1 0.2 convert_add_fusion
  111.3 1.3 convolution_convert_fusion
  112.6 99.1 %all_to_all.25 = bf16[8,8,16,2048]{3,2,1,0:T(8,128)(2,1)S(1)} all-to-all(bf16[8,8,16,2048]{3,2,1,0:T(8,128)(2,1)S(1)} %bitcast.167), channel_id=1, replica_groups=mesh['seq'=8,'tensor'=4] {'seq'}, dimensions={0} | all-to-all | bytes 8388608 | tf_op jit(solution)/shard_map/all_to_all | solution.py:163
  211.8 1.3 fusion.24
  213.0 5.0 %fusion.39 = bf16[8,8,16,256]{3,2,0,1:T(8,128)(2,1)S(1)} fusion(bf16[8,2048,256]{2,1,0:T(8,128)(2,1)} %param.32, bf16[8,8,16,2048]{3,2,1,0:T(8,128)(2,1)S(1)} %all_to_all.25, f32[8,8,16,256]{3,2,0,1:T(8,128)S(1)} %fusion.24), kind=kOutput, calls=%fused_computation.38 | convolution fusion | flops 1075314688 | bytes 14155776 | tf_op jit(solution)/shard_map/gecd,edf->gecf/dot_general | solution.py:18
  218.1 1.3 convert_bitcast_fusion
  219.3 2.5 copy.181
  221.8 4.7 %all-to-all-start.4 = ((bf16[8,8,16,2048]{3,2,1,0:T(8,128)(2,1)}), bf16[8,8,16,2048]{3,2,1,0:T(8,128)(2,1)}, u32[]{:S(2)}, u32[]{:S(2)}) async-start(bf16[8,8,16,2048]{3,2,1,0:T(8,128)(2,1)} %copy.181), calls=%async_computation.4 | async-start | bytes 8388608 | tf_op jit(solution)/shard_map/all_to_all | solution.py:168
  226.6 0.6 gather_fusion
  227.2 0.6 gather_fusion.1
  227.8 0.1 copy.177
  227.8 111.2 %all-gather.2 = bf16[64,1024]{1,0:T(8,128)(2,1)S(1)} all-gather(bf16[8,1024]{1,0:T(8,128)(2,1)S(1)} %pad_maximum_fusion), channel_id=4, replica_groups=mesh['seq'=8,'tensor'=4] {'seq'}, dimensions={0}, use_global_device_ids=true | all-gather | bytes 147456 | tf_op jit(solution)/shard_map/all_gather | solution.py:52
  339.0 0.7 select_reduce_fusion
  339.8 0.3 convolution_convert_fusion.4
  340.1 2.8 convolution_convert_fusion.2
  342.9 3.0 fusion.84
  345.9 3.7 fusion.10
  349.7 4.3 %slice_select_fusion = (bf16[12,128,512]{2,1,0:T(8,128)(2,1)}, bf16[12,128,512]{2,1,0:T(8,128)(2,1)}) fusion(bf16[12,128,512]{2,1,0:T(8,128)(2,1)} %param.22, bf16[12,128,1024]{2,1,0:T(8,128)(2,1)} %convolution_convert_fusion.2, pred[12,128]{1,0:T(8,128)(4,1)S(1)} %fusion.87, bf16[12,128,512]{2,1,0:T(8,128)(2,1)} %param.21), kind=kLoop, calls=%fused_computation.28 | loop fusion | flops 1572864 | bytes 9438720 | tf_op jit(solution)/shard_map/jit(_where)/select_n | solution.py:195
  354.0 13.9 %reduce-scatter.2.cloned.1.call-done = bf16[64,512]{1,0:T(8,128)(2,1)} async-done(((bf16[64,2048]{1,0:T(8,128)(2,1)}), bf16[64,512]{1,0:T(8,128)(2,1)}) %reduce-scatter.2.cloned.1.call-update) | async-done | bytes 65552 | tf_op jit(solution)/shard_map/reduce_scatter | solution.py:175
  368.0 1.5 add_convert_fusion
  (57 shorter events, 0.6 us)
Async XLA Ops:
  7.2 85.3 %copy-start = (bf16[512,2048]{1,0:T(8,128)(2,1)S(1)}, bf16[512,2048]{1,0:T(8,128)(2,1)}, u32[]{:S(2)}) copy-start(bf16[512,2048]{1,0:T(8,128)(2,1)} %param.29) | copy-start | bytes 6291460
  53.5 12.2 %all-to-all-start.2 = ((bf16[8,2,128]{2,1,0:T(2,128)(2,1)}), bf16[8,2,128]{2,1,0:T(2,128)(2,1)S(1)}, u32[]{:S(2)}, u32[]{:S(2)}) async-start(bf16[8,2,128]{2,1,0:T(2,128)(2,1)} %reshape.252), calls=%async_computation.2 | async-start | bytes 8192 | tf_op jit(solution)/shard_map/all_to_all | solution.py:97
  61.6 10.0 %copy-start.6 = (s32[1,64,64]{2,1,0:T(8,128)S(1)}, s32[1,64,64]{2,1,0:T(8,128)}, u32[]{:S(2)}) copy-start(s32[1,64,64]{2,1,0:T(8,128)} %param.26) | copy-start | bytes 49156
  61.7 20.1 %copy-start.3 = (bf16[64,512]{1,0:T(8,128)(2,1)S(1)}, bf16[64,512]{1,0:T(8,128)(2,1)}, u32[]{:S(2)}) copy-start(bf16[64,512]{1,0:T(8,128)(2,1)} %param.18) | copy-start | bytes 196612
  61.7 20.1 %copy-start.4 = (bf16[64,512]{1,0:T(8,128)(2,1)S(1)}, bf16[64,512]{1,0:T(8,128)(2,1)}, u32[]{:S(2)}) copy-start(bf16[64,512]{1,0:T(8,128)(2,1)} %param.19) | copy-start | bytes 196612
  64.9 27.3 %copy-start.5 = (bf16[64,512]{1,0:T(8,128)(2,1)S(1)}, bf16[64,512]{1,0:T(8,128)(2,1)}, u32[]{:S(2)}) copy-start(bf16[64,512]{1,0:T(8,128)(2,1)} %param.20) | copy-start | bytes 196612
  65.7 12.5 %all-to-all-start = ((bf16[8,2,128]{2,1,0:T(2,128)(2,1)}), bf16[8,2,128]{2,1,0:T(2,128)(2,1)S(1)}, u32[]{:S(2)}, u32[]{:S(2)}) async-start(bf16[8,2,128]{2,1,0:T(2,128)(2,1)} %reshape.250), calls=%async_computation | async-start | bytes 8192 | tf_op jit(solution)/shard_map/all_to_all | solution.py:94
  78.2 13.7 %all-to-all-start.1 = ((bf16[8,4,64,128]{3,2,1,0:T(8,128)(2,1)}), bf16[8,4,64,128]{3,2,1,0:T(8,128)(2,1)S(1)}, u32[]{:S(2)}, u32[]{:S(2)}) async-start(bf16[8,4,64,128]{3,2,1,0:T(8,128)(2,1)} %copy.170), calls=%async_computation.1 | async-start | bytes 1048576 | tf_op jit(solution)/shard_map/all_to_all | solution.py:91
  81.7 28.0 %all-gather.5.cloned.1.call-start = ((), (), s32[]{:S(2)}) async-start(), calls=%async_computation.7 | async-start | bytes 1310720 | tf_op jit(solution)/shard_map/all_gather | solution.py:135
  82.0 11.7 %copy-start.7 = (s32[64,8]{0,1:T(8,128)S(1)}, s32[64,8]{0,1:T(8,128)}, u32[]{:S(2)}) copy-start(s32[64,8]{0,1:T(8,128)} %param.34) | copy-start | bytes 6148
  92.5 18.6 %copy-start.2 = (bf16[64,2048]{1,0:T(8,128)(2,1)S(1)}, bf16[64,2048]{1,0:T(8,128)(2,1)}, u32[]{:S(2)}) copy-start(bf16[64,2048]{1,0:T(8,128)(2,1)} %param.28) | copy-start | bytes 786436
  93.7 17.6 %copy-start.8 = (f32[2048]{0:T(1024)S(1)}, f32[2048]{0:T(1024)}, u32[]{:S(2)}) copy-start(f32[2048]{0:T(1024)} %param.30) | copy-start | bytes 24580
  111.3 100.5 %slice-start.2 = ((s8[8388608]{0:T(1024)(128)(4,1)}), s8[4194304]{0:T(1024)(128)(4,1)S(1)}, s32[]{:S(2)}) async-start(s8[8388608]{0:T(1024)(128)(4,1)} %bitcast.175), calls=%async_computation.10 | async-start | bytes 8388608
  112.6 99.1 %slice-start.3 = ((s8[8388608]{0:T(1024)(128)(4,1)}), s8[4194304]{0:T(1024)(128)(4,1)S(1)}, s32[]{:S(2)}) async-start(s8[8388608]{0:T(1024)(128)(4,1)} %bitcast.175), calls=%async_computation.11 | async-start | bytes 8388608
  211.8 6.3 %slice-start = ((s8[8388608]{0:T(1024)(128)(4,1)}), s8[4194304]{0:T(1024)(128)(4,1)S(1)}, s32[]{:S(2)}) async-start(s8[8388608]{0:T(1024)(128)(4,1)} %bitcast.168), calls=%async_computation.8 | async-start | bytes 8388608
  213.0 5.0 %slice-start.1 = ((s8[8388608]{0:T(1024)(128)(4,1)}), s8[4194304]{0:T(1024)(128)(4,1)S(1)}, s32[]{:S(2)}) async-start(s8[8388608]{0:T(1024)(128)(4,1)} %bitcast.168), calls=%async_computation.9 | async-start | bytes 8388608
  221.8 4.7 %copy-start.11 = (s32[1,8]{1,0:T(1,128)S(1)}, s32[1,8]{1,0:T(1,128)}, u32[]{:S(2)}) copy-start(s32[1,8]{1,0:T(1,128)} %param.27) | copy-start | bytes 100
  221.8 5.9 %copy-start.9 = (f32[64,8]{0,1:T(8,128)S(1)}, f32[64,8]{0,1:T(8,128)}, u32[]{:S(2)}) copy-start(f32[64,8]{0,1:T(8,128)} %param.35) | copy-start | bytes 6148
  221.8 118.0 %copy-start.10 = (s32[12]{0:T(128)S(1)}, s32[12]{0:T(128)}, u32[]{:S(2)}) copy-start(s32[12]{0:T(128)} %param.23) | copy-start | bytes 148
  221.8 121.1 %all-to-all-start.4 = ((bf16[8,8,16,2048]{3,2,1,0:T(8,128)(2,1)}), bf16[8,8,16,2048]{3,2,1,0:T(8,128)(2,1)}, u32[]{:S(2)}, u32[]{:S(2)}) async-start(bf16[8,8,16,2048]{3,2,1,0:T(8,128)(2,1)} %copy.181), calls=%async_computation.4 | async-start | bytes 8388608 | tf_op jit(solution)/shard_map/all_to_all | solution.py:168
  226.5 141.5 %reduce-scatter.2.cloned.1.call-start = ((), (), s32[]{:S(2)}) async-start(), calls=%async_computation.6 | async-start | bytes 327680 | tf_op jit(solution)/shard_map/reduce_scatter | solution.py:175
  349.7 19.7 %copy-start.1 = (bf16[512,2048]{1,0:T(8,128)(2,1)S(1)}, bf16[512,2048]{1,0:T(8,128)(2,1)}, u32[]{:S(2)}) copy-start(bf16[512,2048]{1,0:T(8,128)(2,1)} %param.29) | copy-start | bytes 6291460
Sparse Core Ops, SparseCore 0:
  93.8 15.8 all-gather.4
  349.8 18.1 reduce-scatter.1
